TPU v7x, 256 devices: a whole 4x4x8 slice. The times are simulated.
256 devices in a mesh: band: 8 (over x, core), dom: 32 (over z, y).
Axes of the slice: x: 4, y: 4, z: 8, core: 2. Of those that a mesh axis runs over, the one named last changes fastest.
Arguments:
- orbitals: bfloat16 [256, 192, 48, 64], P('band', 'dom'), may hold values from -1.796875 to 1.796875
- potential: float32 [192, 48, 64], P('dom'), may hold values from -2 to 1
- projectors: float32 [2048, 128], P('dom'), may hold values from -1.5 to 1.5
- coupling: float32 [1024], P('dom'), may hold values from 0.5 to 2
- slot_block: int32 [2048], P('dom'), may hold values from 0 to 143
- slot_projector: int32 [2048], P('dom'), may hold values from 0 to 1023, as said below
- slot_count: int32 [32], P('dom'), may hold values from 16 to 64, as said below
- locked: bfloat16 [2048, 192, 3072], P(None, 'dom', 'band'), may hold values from -0.0078125 to 0.0078125
Outputs:
- orthogonal: bfloat16 [256, 192, 3072], P(None, 'dom', 'band')
- margins: float32 [2048, 256], P(('band', 'dom'))
Inputs may be any that keep to these rules, and one draw needn't show every extreme that they name: `slot_projector`: projector p belongs to domain p // 32; a slot of domain d names a projector of domain d - 1, d or d + 1, cyclically; slot 0 of every domain names one of domain d - 1 and slot 1 one of domain d + 1. The used slots of a domain are its first slot_count slots; some domain uses all and some uses 64 // 4.
All inputs are finite; a program needn't handle non-finite values.
Results may differ from a plain program's by a relative error of at most 0.0039.
The roundings to bfloat16 on the way count: a program that leaves them out, or rounds other values in their place, can miss the bound.
Values may be sent and summed in bfloat16 or wider, within the bound.
No kernel may reach another device: no remote copies, remote signals or barrier semaphores. Data moves between devices by JAX's collectives and lax.ppermute only.
A program may use at most 320 MiB of HBM per device.

v0:
```python
import jax
import jax.numpy as jnp
from jax import lax
from jax.sharding import PartitionSpec as P

BS = 128
PROJ_DOM = 32
COEFFS = (
    -5369.0 / 1800.0,
    12.0 / 7.0,
    -15.0 / 56.0,
    10.0 / 189.0,
    -1.0 / 112.0,
    2.0 / 825.0,
    -1.0 / 5544.0,
)


def with_halo(shard, sides, width):
    for axis, dim in sides:
        size, length = (lax.axis_size(axis), shard.shape[dim])
        up = [(i, (i + 1) % size) for i in range(size)]
        down = [(j, i) for i, j in up]
        last = lax.slice_in_dim(shard, length - width, length, axis=dim)
        initial = lax.slice_in_dim(shard, 0, width, axis=dim)
        before = lax.ppermute(last, axis, up)
        after = lax.ppermute(initial, axis, down)
        shard = jnp.concatenate([before, shard, after], axis=dim)
    return shard


def laplacian(orbital, extended):
    planes_x = orbital.shape[1]
    depth_z = orbital.shape[2]
    laplace = 3.0 * COEFFS[0] * orbital
    padded = jnp.pad(orbital, ((0, 0), (0, 0), (6, 6), (0, 0)))
    for offset in range(1, 7):
        weight = COEFFS[offset]
        laplace = laplace + weight * (
            extended[:, 6 + offset : 6 + offset + planes_x]
            + extended[:, 6 - offset : 6 - offset + planes_x]
        )
        laplace = laplace + weight * (jnp.roll(orbital, offset, 3) + jnp.roll(orbital, -offset, 3))
        laplace = laplace + weight * (
            padded[:, :, 6 + offset : 6 + offset + depth_z]
            + padded[:, :, 6 - offset : 6 - offset + depth_z]
        )
    return laplace


def per_device(
    orbitals, potential, projectors, coupling, slot_block, slot_projector, slot_count, locked
):
    orbital = orbitals.astype(jnp.float32)
    extended = with_halo(orbitals, (("dom", 1),), 6).astype(jnp.float32)
    laplace = laplacian(orbital, extended)
    band_rows, planes_x, depth_z, width_y = orbital.shape
    blocks_count = planes_x * depth_z * width_y // BS
    flat = orbital.reshape(band_rows, blocks_count, BS)
    blocks = flat[:, slot_block]
    slots = slot_block.shape[0]
    active = (jnp.arange(slots, dtype=jnp.int32) < slot_count[0]).astype(jnp.float32)
    inner_part = jnp.sum(blocks * projectors[None], axis=2) * active[None]
    domains = lax.axis_size("dom")
    here = lax.axis_index("dom")
    owner = slot_projector // PROJ_DOM
    local_id = slot_projector % PROJ_DOM
    relative = (owner - here + domains) % domains
    column = jnp.where(
        relative == 0,
        PROJ_DOM + local_id,
        jnp.where(relative == 1, 2 * PROJ_DOM + local_id, local_id),
    )
    onehot = (column[:, None] == jnp.arange(3 * PROJ_DOM, dtype=jnp.int32)[None, :]).astype(
        jnp.float32
    )
    partial_value = jnp.dot(inner_part, onehot, precision=lax.Precision.HIGHEST)
    outgoing = jnp.concatenate(
        [partial_value[:, :PROJ_DOM], partial_value[:, 2 * PROJ_DOM :]], axis=1
    )
    arrived = with_halo(outgoing, (("dom", 1),), PROJ_DOM)
    owned = (
        partial_value[:, PROJ_DOM : 2 * PROJ_DOM] + arrived[:, :PROJ_DOM] + arrived[:, -PROJ_DOM:]
    )
    table_local = owned * coupling[None]
    table = with_halo(table_local, (("dom", 1),), PROJ_DOM)
    slot_value = jnp.dot(table, onehot.T, precision=lax.Precision.HIGHEST) * active[None]
    contribution = slot_value[:, :, None] * projectors[None]
    nonlocal_term = jnp.zeros_like(flat).at[:, slot_block].add(contribution).reshape(orbital.shape)
    hamilton = -0.5 * laplace + potential[None] * orbital + nonlocal_term
    numerator, denominator = lax.psum(
        (jnp.sum(orbital * hamilton, axis=(1, 2, 3)), jnp.sum(orbital * orbital, axis=(1, 2, 3))),
        "dom",
    )
    energy = numerator / denominator
    residual = (hamilton - energy[:, None, None, None] * orbital).astype(jnp.bfloat16)
    residual = residual.reshape(band_rows, planes_x, depth_z * width_y)
    moved = lax.all_to_all(residual, "band", split_axis=2, concat_axis=0, tiled=True)
    all_bands = moved.shape[0]
    locked_flat = locked.reshape(locked.shape[0], -1)
    residual_flat = moved.reshape(all_bands, -1)
    contract_cells = (((1,), (1,)), ((), ()))
    share_rows = locked.shape[0] // lax.axis_size(("band", "dom"))
    summed = lax.psum(
        lax.dot_general(
            locked_flat, residual_flat, contract_cells, preferred_element_type=jnp.float32
        ),
        ("band", "dom"),
    )
    margins = lax.dynamic_slice_in_dim(
        summed, lax.axis_index(("band", "dom")) * share_rows, share_rows, 0
    )
    coeffs = summed.astype(jnp.bfloat16)
    correction = lax.dot_general(
        coeffs, locked_flat, (((0,), (0,)), ((), ())), preferred_element_type=jnp.float32
    )
    orthogonal = (
        (residual_flat.astype(jnp.float32) - correction).astype(jnp.bfloat16).reshape(moved.shape)
    )
    return (orthogonal, margins)


def solution(mesh):
    in_specs = (
        P("band", "dom", None, None),
        P("dom", None, None),
        P("dom", None),
        P("dom"),
        P("dom"),
        P("dom"),
        P("dom"),
        P(None, "dom", "band"),
    )
    out_specs = (P(None, "dom", "band"), P(("band", "dom"), None))
    return jax.shard_map(
        per_device, mesh=mesh, in_specs=in_specs, out_specs=out_specs, check_vma=False
    )
```

profile of v0, /device:TPU:2, one launch (start us, length us, event | category | flops | bytes accessed | tf_op | source)
XLA Modules:
  0.0 610.1 jit_solution(6926809845291708726)
XLA Ops:
  8.8 6.8 %collective-permute-start.1 = (bf16[32,6,48,64]{3,2,1,0:T(8,128)(2,1)}, bf16[32,6,48,64]{3,2,1,0:T(8,128)(2,1)}, u32[]{:S(2)}, u32[]{:S(2)}) collective-permute-start(bf16[32,6,48,64]{3,2,1,0:T(8,128)(2,1)} %param.8), channel_id=1, source_target_pairs={{1,0},{2,1},{3,2},{4,3},{5,4},{6,5},{7,6},{8,7},{9,8},{10,9},{11,1... | collective-permute-start | bytes 3538952 | tf_op jit(solution)/shard_map/ppermute | solution.py:27
  15.7 4.4 reshape.34
  27.8 5.8 collective-permute-start.3
  33.5 4.6 fusion.65
  38.1 4.7 fusion.66
  42.8 4.7 fusion.67
  47.5 4.6 fusion.68
  52.1 4.6 fusion.69
  56.8 4.6 fusion.70
  61.3 4.7 fusion.71
  66.0 4.6 fusion.72
  70.6 4.6 fusion.73
  75.2 4.7 fusion.74
  79.9 4.6 fusion.75
  84.7 5.5 collective-permute-start.5
  90.2 4.7 fusion.76
  99.9 8.0 %scatter_fusion = f32[32,144,128]{2,0,1:T(8,128)} fusion(f32[32,144,128]{2,0,1:T(8,128)} %broadcast_in_dim.4, s32[64]{0:T(128)S(1)} %compare_select_fusion, f32[64,32,128]{2,1,0:T(8,128)S(1)} %multiply_bitcast_fusion), kind=kCustom, calls=%fused_computation.1 | custom fusion | flops 262144 | bytes 3145984 | tf_op jit(solution)/shard_map/scatter-add | solution.py:89
  108.0 4.5 copy.32
  112.4 4.5 reshape.35
  117.0 8.1 %maximum_convert_fusion = f32[32,18,48,64]{3,2,1,0:T(8,128)} fusion(bf16[32,6,48,64]{3,2,1,0:T(8,128)(2,1)} %collective-permute-done.1, bf16[32,6,48,64]{3,2,1,0:T(8,128)(2,1)S(1)} %copy-done, bf16[32,6,48,64]{3,2,1,0:T(8,128)(2,1)} %collective-permute-done), kind=kLoop, calls=%fused_computation.14 | loop fusion | flops 5308416 | bytes 10616832 | tf_op jit(solution)/shard_map/convert_element_type | solution.py:55
  125.1 75.7 %fusion.21 = (f32[32]{0:T(128)S(1)}, f32[32]{0:T(128)S(1)}, f32[32,6,48,64]{3,2,1,0:T(8,128)}) fusion(bf16[32,6,48,64]{3,2,1,0:T(8,128)(2,1)S(1)} %copy-done, f32[32,6,48,64]{3,2,1,0:T(8,128)} %reshape.35, f32[6,48,64]{2,1,0:T(8,128)S(1)} %copy-done.1, f32[32,6,48,6]{3,2,1,0:T(8,128)} %get-tuple-element.36, f32[32,6,48,58]{3,2,1,0:T(8,128)} %get-tuple-element.38, ...), kind=kLoop, calls=%fused_computation.41 | loop fusion | flops 44826560 | bytes 64954624 | tf_op jit(solution)/shard_map/reduce_sum | solution.py:92
  200.8 69.9 %all-reduce.1 = (f32[32]{0:T(128)S(1)}, f32[32]{0:T(128)S(1)}) all-reduce(f32[32]{0:T(128)S(1)} %get-tuple-element.11, f32[32]{0:T(128)S(1)} %get-tuple-element.10), channel_id=1, replica_groups=mesh['band'=8,'dom'=32] {'dom'}, use_global_device_ids=true, to_apply=%region_3.4 | all-reduce | flops 64 | bytes 512 | tf_op jit(solution)/shard_map/psum | solution.py:91
  270.7 4.6 fusion.23
  275.2 7.8 %copy.45 = bf16[32,6,48,64]{0,1,3,2:T(8,128)(2,1)} copy(bf16[32,6,48,64]{3,2,1,0:T(8,128)(2,1)} %fusion.23) | data formatting | bytes 2359296 | tf_op jit(solution)/shard_map/reshape | solution.py:97
  283.0 8.6 %reshape.59 = bf16[8,2,36864]{2,1,0:T(2,128)(2,1)} reshape(bf16[3072,6,32]{2,1,0:T(8,128)(2,1)} %bitcast.23) | data formatting | bytes 2359296
  291.6 4.8 all-to-all-start
  296.5 12.5 %copy.37 = bf16[2048,6,384]{0,2,1:T(8,128)(2,1)} copy(bf16[2048,6,384]{2,0,1:T(8,128)(2,1)} %param.15) | data formatting | bytes 18874368 | tf_op args[7]
  312.4 6.2 %reshape.60 = bf16[3072,6,32]{2,1,0:T(8,128)(2,1)} reshape(bf16[8,2,36864]{2,1,0:T(2,128)(2,1)S(1)} %all-to-all-done) | data formatting | bytes 2359296
  318.5 6.5 %copy.36 = bf16[8,32,6,384]{3,2,1,0:T(8,128)(2,1)S(1)} copy(bf16[8,32,6,384]{1,2,3,0:T(8,128)(2,1)} %bitcast.24) | data formatting | bytes 2359296 | tf_op jit(solution)/shard_map/all_to_all | solution.py:98
  325.2 7.7 %convolution_bitcast_fusion = f32[2048,256]{0,1:T(8,128)} fusion(bf16[256,2304]{1,0:T(8,128)(2,1)S(1)} %bitcast.29, bf16[2048,2304]{0,1:T(8,128)(2,1)} %bitcast.25), kind=kOutput, calls=%fused_computation.82 | convolution fusion | flops 2415919104 | bytes 12713984 | tf_op jit(solution)/shard_map/dot_general | solution.py:105
  333.0 259.3 %all-reduce.4.cloned.1.call-done = f32[2048,256]{0,1:T(8,128)} async-done(((f32[2048,256]{0,1:T(8,128)}), f32[2048,256]{0,1:T(8,128)}) %all-reduce.4.cloned.1.call-update) | async-done | bytes 2097168 | tf_op jit(solution)/shard_map/psum | solution.py:104
  592.3 7.0 %fusion.48 = bf16[256,2304]{1,0:T(8,128)(2,1)S(1)} fusion(bf16[2048,2304]{0,1:T(8,128)(2,1)} %bitcast.26, bf16[256,2304]{1,0:T(8,128)(2,1)S(1)} %bitcast.30, f32[2048,256]{0,1:T(8,128)} %all-reduce.4.cloned.1.call-done), kind=kOutput, calls=%fused_computation.81 | convolution fusion | flops 2418212864 | bytes 13893632 | tf_op jit(solution)/shard_map/dot_general | solution.py:114
  (45 shorter events, 21.1 us)
Async XLA Ops:
  7.2 12.9 %copy-start.4 = (s32[64]{0:T(128)S(1)}, s32[64]{0:T(128)}, u32[]{:S(2)}) copy-start(s32[64]{0:T(128)} %param.12) | copy-start | bytes 772
  7.2 109.8 %collective-permute-start = (bf16[32,6,48,64]{3,2,1,0:T(8,128)(2,1)}, bf16[32,6,48,64]{3,2,1,0:T(8,128)(2,1)}, u32[]{:S(2)}, u32[]{:S(2)}) collective-permute-start(bf16[32,6,48,64]{3,2,1,0:T(8,128)(2,1)} %param.8), channel_id=1, source_target_pairs={{0,1},{1,2},{2,3},{3,4},{4,5},{5,6},{6,7},{7,8},{8,9},{9,10},{10,1... | collective-permute-start | bytes 3538952 | tf_op jit(solution)/shard_map/ppermute | solution.py:26
  8.8 108.2 %collective-permute-start.1 = (bf16[32,6,48,64]{3,2,1,0:T(8,128)(2,1)}, bf16[32,6,48,64]{3,2,1,0:T(8,128)(2,1)}, u32[]{:S(2)}, u32[]{:S(2)}) collective-permute-start(bf16[32,6,48,64]{3,2,1,0:T(8,128)(2,1)} %param.8), channel_id=1, source_target_pairs={{1,0},{2,1},{3,2},{4,3},{5,4},{6,5},{7,6},{8,7},{9,8},{10,9},{11,1... | collective-permute-start | bytes 3538952 | tf_op jit(solution)/shard_map/ppermute | solution.py:27
  15.7 9.1 %copy-start.5 = (s32[64]{0:T(128)S(1)}, s32[64]{0:T(128)}, u32[]{:S(2)}) copy-start(s32[64]{0:T(128)} %param.13) | copy-start | bytes 772
  15.7 11.4 %copy-start.2 = (f32[64,128]{1,0:T(8,128)S(1)}, f32[64,128]{1,0:T(8,128)}, u32[]{:S(2)}) copy-start(f32[64,128]{1,0:T(8,128)} %param.10) | copy-start | bytes 98308
  20.0 13.5 %copy-start = (bf16[32,6,48,64]{3,2,1,0:T(8,128)(2,1)S(1)}, bf16[32,6,48,64]{3,2,1,0:T(8,128)(2,1)}, u32[]{:S(2)}) copy-start(bf16[32,6,48,64]{3,2,1,0:T(8,128)(2,1)} %param.8) | copy-start | bytes 3538948
  27.7 56.8 %collective-permute-start.2 = (f32[32,32]{1,0:T(8,128)S(1)}, f32[32,32]{1,0:T(8,128)S(1)}, u32[]{:S(2)}, u32[]{:S(2)}) collective-permute-start(f32[32,32]{1,0:T(8,128)S(1)} %get-tuple-element.39), channel_id=1, source_target_pairs={{0,1},{1,2},{2,3},{3,4},{4,5},{5,6},{6,7},{7,8},{8,9},{9,10},{10,1... | collective-permute-start | bytes 12296 | tf_op jit(solution)/shard_map/ppermute | solution.py:26
  27.8 56.8 %collective-permute-start.3 = (f32[32,32]{1,0:T(8,128)S(1)}, f32[32,32]{1,0:T(8,128)S(1)}, u32[]{:S(2)}, u32[]{:S(2)}) collective-permute-start(f32[32,32]{1,0:T(8,128)S(1)} %get-tuple-element.40), channel_id=1, source_target_pairs={{1,0},{2,1},{3,2},{4,3},{5,4},{6,5},{7,6},{8,7},{9,8},{10,9},{11,1... | collective-permute-start | bytes 12296 | tf_op jit(solution)/shard_map/ppermute | solution.py:27
  79.9 4.7 copy-start.3
  84.6 12.9 %collective-permute-start.4 = (f32[32,32]{1,0:T(8,128)S(1)}, f32[32,32]{1,0:T(8,128)S(1)}, u32[]{:S(2)}, u32[]{:S(2)}) collective-permute-start(f32[32,32]{1,0:T(8,128)S(1)} %fusion.53), channel_id=1, source_target_pairs={{0,1},{1,2},{2,3},{3,4},{4,5},{5,6},{6,7},{7,8},{8,9},{9,10},{10,1... | collective-permute-start | bytes 12296 | tf_op jit(solution)/shard_map/ppermute | solution.py:26
  84.7 12.9 %collective-permute-start.5 = (f32[32,32]{1,0:T(8,128)S(1)}, f32[32,32]{1,0:T(8,128)S(1)}, u32[]{:S(2)}, u32[]{:S(2)}) collective-permute-start(f32[32,32]{1,0:T(8,128)S(1)} %fusion.53), channel_id=1, source_target_pairs={{1,0},{2,1},{3,2},{4,3},{5,4},{6,5},{7,6},{8,7},{9,8},{10,9},{11,1... | collective-permute-start | bytes 12296 | tf_op jit(solution)/shard_map/ppermute | solution.py:27
  117.0 8.1 %copy-start.1 = (f32[6,48,64]{2,1,0:T(8,128)S(1)}, f32[6,48,64]{2,1,0:T(8,128)}, u32[]{:S(2)}) copy-start(f32[6,48,64]{2,1,0:T(8,128)} %param.9) | copy-start | bytes 221188
  291.6 20.7 %all-to-all-start = ((bf16[8,2,36864]{2,1,0:T(2,128)(2,1)}), bf16[8,2,36864]{2,1,0:T(2,128)(2,1)S(1)}, u32[]{:S(2)}, u32[]{:S(2)}) async-start(bf16[8,2,36864]{2,1,0:T(2,128)(2,1)} %reshape.59), calls=%async_computation | async-start | bytes 2359296 | tf_op jit(solution)/shard_map/all_to_all | solution.py:98
  296.5 295.9 %all-reduce.4.cloned.1.call-start = ((), (), s32[]{:S(2)}) async-start(), calls=%async_computation.1 | async-start | bytes 4194304 | tf_op jit(solution)/shard_map/psum | solution.py:104
Sparse Core Ops, SparseCore 0:
  333.1 259.1 all-reduce.3
where the time goes:
time: 616 us; the launch traced here: 610 us
  waiting for transfers between devices  263 us (43%)
  local copies, waits for them, and re-layouts  123 us (20%)
  other arithmetic  99.9 us (16%)
  blocking collectives  69.9 us (11%)
  starting transfers between devices  24.7 us (4%)
  matrix products  15.2 us (2%)
  between operations  15.1 us (2%)
    psum x1, waiting for transfers between devices, per_device(): lax.psum(lax.dot_general(locked_flat, residual_flat, contract_cells, pref...  259 us
    reduce_sum x1, other arithmetic, per_device(): jnp.sum(orbital * orbital, axis=(1, 2, 3))  75.7 us
    psum x1, blocking collectives, per_device(): lax.psum((jnp.sum(orbital * hamilton, axis=(1, 2, 3)), jnp.sum(orbital *...  69.9 us
    slice x12, local copies, waits for them, and re-layouts, laplacian(): jnp.roll(orbital, offset, 3) + jnp.roll(orbital, -offset, 3)  55.6 us
    unnamed x18, local copies, waits for them, and re-layouts  29.6 us
    ppermute x3, starting transfers between devices, with_halo(): after = lax.ppermute(initial, axis, down)  18.1 us
  transfers between devices with their start and end apart: 8, of which 2 were waited for; matrix products, arithmetic and copies ran while one was open for 17% of the time, Pallas kernels for 0%

commit v1 on v0

--- a/solution.py
+++ b/solution.py
@@ -14,6 +14,11 @@
     2.0 / 825.0,
     -1.0 / 5544.0,
 )
+
+
+def one_after_other(x, axis_one, axis_two):
+    half = lax.psum(x, axis_one)
+    return lax.psum(half, axis_two)
 
 
 def with_halo(shard, sides, width):
@@ -101,11 +106,12 @@
     residual_flat = moved.reshape(all_bands, -1)
     contract_cells = (((1,), (1,)), ((), ()))
     share_rows = locked.shape[0] // lax.axis_size(("band", "dom"))
-    summed = lax.psum(
+    summed = one_after_other(
         lax.dot_general(
             locked_flat, residual_flat, contract_cells, preferred_element_type=jnp.float32
         ),
-        ("band", "dom"),
+        "dom",
+        "band",
     )
     margins = lax.dynamic_slice_in_dim(
         summed, lax.axis_index(("band", "dom")) * share_rows, share_rows, 0

time: 616 us -> 579 us (0.940)
  waiting for transfers between devices: 263 us -> 223 us
    psum x1 -> x2, waiting for transfers between devices: 259 us -> 220 us  [the longest x1 152 us: one_after_other(): half = lax.psum(x, axis_one)]
  transfers between devices with their start and end apart: 8 -> 9, of which waited for: 2 -> 3; matrix products, arithmetic and copies ran while one was open for 17% -> 18% of each run, Pallas kernels for 0% -> 0%
where the time goes in v1:
time: 579 us; the launch traced here: 571 us
  waiting for transfers between devices  223 us (39%)
  local copies, waits for them, and re-layouts  123 us (21%)
  other arithmetic  99.9 us (17%)
  blocking collectives  69.9 us (12%)
  starting transfers between devices  24.7 us (4%)
  matrix products  15.2 us (3%)
  between operations  15.1 us (3%)
    psum x1, waiting for transfers between devices, one_after_other(): half = lax.psum(x, axis_one)  152 us
    reduce_sum x1, other arithmetic, per_device(): jnp.sum(orbital * orbital, axis=(1, 2, 3))  75.7 us
    psum x1, blocking collectives, per_device(): lax.psum((jnp.sum(orbital * hamilton, axis=(1, 2, 3)), jnp.sum(orbital *...  69.9 us
    psum x1, waiting for transfers between devices, one_after_other(): return lax.psum(half, axis_two)  67.7 us
    slice x12, local copies, waits for them, and re-layouts, laplacian(): jnp.roll(orbital, offset, 3) + jnp.roll(orbital, -offset, 3)  55.6 us
    unnamed x18, local copies, waits for them, and re-layouts  29.6 us
    ppermute x3, starting transfers between devices, with_halo(): after = lax.ppermute(initial, axis, down)  18.1 us
  transfers between devices with their start and end apart: 9, of which 3 were waited for; matrix products, arithmetic and copies ran while one was open for 18% of the time, Pallas kernels for 0%

profile of v1, /device:TPU:2, one launch (start us, length us, event | category | flops | bytes accessed | tf_op | source)
XLA Modules:
  0.0 570.7 jit_solution(17742313811567750889)
XLA Ops:
  8.8 6.8 %collective-permute-start.1 = (bf16[32,6,48,64]{3,2,1,0:T(8,128)(2,1)}, bf16[32,6,48,64]{3,2,1,0:T(8,128)(2,1)}, u32[]{:S(2)}, u32[]{:S(2)}) collective-permute-start(bf16[32,6,48,64]{3,2,1,0:T(8,128)(2,1)} %param.8), channel_id=1, source_target_pairs={{1,0},{2,1},{3,2},{4,3},{5,4},{6,5},{7,6},{8,7},{9,8},{10,9},{11,1... | collective-permute-start | bytes 3538952 | tf_op jit(solution)/shard_map/ppermute | solution.py:32
  27.8 5.8 %collective-permute-start.3 = (f32[32,32]{1,0:T(8,128)S(1)}, f32[32,32]{1,0:T(8,128)S(1)}, u32[]{:S(2)}, u32[]{:S(2)}) collective-permute-start(f32[32,32]{1,0:T(8,128)S(1)} %get-tuple-element.40), channel_id=1, source_target_pairs={{1,0},{2,1},{3,2},{4,3},{5,4},{6,5},{7,6},{8,7},{9,8},{10,9},{11,1... | collective-permute-start | bytes 12296 | tf_op jit(solution)/shard_map/ppermute | solution.py:32
  33.5 4.6 fusion.65
  38.1 4.7 fusion.66
  42.8 4.7 fusion.67
  47.5 4.6 fusion.68
  52.1 4.6 fusion.69
  56.8 4.6 fusion.70
  61.3 4.7 fusion.71
  66.0 4.6 fusion.72
  70.6 4.6 fusion.73
  75.2 4.7 fusion.74
  79.9 4.6 fusion.75
  84.7 5.5 collective-permute-start.5
  90.2 4.7 fusion.76
  99.9 8.0 %scatter_fusion = f32[32,144,128]{2,0,1:T(8,128)} fusion(f32[32,144,128]{2,0,1:T(8,128)} %broadcast_in_dim.4, s32[64]{0:T(128)S(1)} %compare_select_fusion, f32[64,32,128]{2,1,0:T(8,128)S(1)} %multiply_bitcast_fusion), kind=kCustom, calls=%fused_computation.1 | custom fusion | flops 262144 | bytes 3145984 | tf_op jit(solution)/shard_map/scatter-add | solution.py:94
  108.0 4.5 copy.32
  112.4 4.5 reshape.35
  117.0 8.1 %maximum_convert_fusion = f32[32,18,48,64]{3,2,1,0:T(8,128)} fusion(bf16[32,6,48,64]{3,2,1,0:T(8,128)(2,1)} %collective-permute-done.1, bf16[32,6,48,64]{3,2,1,0:T(8,128)(2,1)S(1)} %copy-done, bf16[32,6,48,64]{3,2,1,0:T(8,128)(2,1)} %collective-permute-done), kind=kLoop, calls=%fused_computation.14 | loop fusion | flops 5308416 | bytes 10616832 | tf_op jit(solution)/shard_map/convert_element_type | solution.py:60
  125.1 75.7 %fusion.21 = (f32[32]{0:T(128)S(1)}, f32[32]{0:T(128)S(1)}, f32[32,6,48,64]{3,2,1,0:T(8,128)}) fusion(bf16[32,6,48,64]{3,2,1,0:T(8,128)(2,1)S(1)} %copy-done, f32[32,6,48,64]{3,2,1,0:T(8,128)} %reshape.35, f32[6,48,64]{2,1,0:T(8,128)S(1)} %copy-done.1, f32[32,6,48,6]{3,2,1,0:T(8,128)} %get-tuple-element.36, f32[32,6,48,58]{3,2,1,0:T(8,128)} %get-tuple-element.38, ...), kind=kLoop, calls=%fused_computation.41 | loop fusion | flops 44826560 | bytes 64954624 | tf_op jit(solution)/shard_map/reduce_sum | solution.py:97
  200.8 69.9 %all-reduce.1 = (f32[32]{0:T(128)S(1)}, f32[32]{0:T(128)S(1)}) all-reduce(f32[32]{0:T(128)S(1)} %get-tuple-element.11, f32[32]{0:T(128)S(1)} %get-tuple-element.10), channel_id=1, replica_groups=mesh['band'=8,'dom'=32] {'dom'}, use_global_device_ids=true, to_apply=%region_3.4 | all-reduce | flops 64 | bytes 512 | tf_op jit(solution)/shard_map/psum | solution.py:96
  270.7 4.6 fusion.23
  275.2 7.8 %copy.45 = bf16[32,6,48,64]{0,1,3,2:T(8,128)(2,1)} copy(bf16[32,6,48,64]{3,2,1,0:T(8,128)(2,1)} %fusion.23) | data formatting | bytes 2359296 | tf_op jit(solution)/shard_map/reshape | solution.py:102
  283.0 8.6 %reshape.59 = bf16[8,2,36864]{2,1,0:T(2,128)(2,1)} reshape(bf16[3072,6,32]{2,1,0:T(8,128)(2,1)} %bitcast.23) | data formatting | bytes 2359296
  291.6 4.8 all-to-all-start
  296.5 12.5 %copy.37 = bf16[2048,6,384]{0,2,1:T(8,128)(2,1)} copy(bf16[2048,6,384]{2,0,1:T(8,128)(2,1)} %param.15) | data formatting | bytes 18874368 | tf_op args[7]
  312.4 6.2 %reshape.60 = bf16[3072,6,32]{2,1,0:T(8,128)(2,1)} reshape(bf16[8,2,36864]{2,1,0:T(2,128)(2,1)S(1)} %all-to-all-done) | data formatting | bytes 2359296
  318.5 6.5 %copy.36 = bf16[8,32,6,384]{3,2,1,0:T(8,128)(2,1)S(1)} copy(bf16[8,32,6,384]{1,2,3,0:T(8,128)(2,1)} %bitcast.24) | data formatting | bytes 2359296 | tf_op jit(solution)/shard_map/all_to_all | solution.py:103
  325.2 7.7 %convolution_bitcast_fusion = f32[2048,256]{0,1:T(8,128)} fusion(bf16[256,2304]{1,0:T(8,128)(2,1)S(1)} %bitcast.29, bf16[2048,2304]{0,1:T(8,128)(2,1)} %bitcast.25), kind=kOutput, calls=%fused_computation.82 | convolution fusion | flops 2415919104 | bytes 12713984 | tf_op jit(solution)/shard_map/dot_general | solution.py:110
  333.1 152.2 %all-reduce.5.cloned.1.call-done = f32[2048,256]{0,1:T(8,128)} async-done(((f32[2048,256]{0,1:T(8,128)}), f32[2048,256]{0,1:T(8,128)}) %all-reduce.5.cloned.1.call-update) | async-done | bytes 2097168 | tf_op jit(solution)/shard_map/psum | solution.py:20
  485.3 67.7 %all-reduce.7.cloned.1.call-done = f32[2048,256]{0,1:T(8,128)} async-done(((f32[2048,256]{0,1:T(8,128)}), f32[2048,256]{0,1:T(8,128)}) %all-reduce.7.cloned.1.call-update) | async-done | bytes 2097168 | tf_op jit(solution)/shard_map/psum | solution.py:21
  552.9 7.0 %fusion.48 = bf16[256,2304]{1,0:T(8,128)(2,1)S(1)} fusion(bf16[2048,2304]{0,1:T(8,128)(2,1)} %bitcast.26, bf16[256,2304]{1,0:T(8,128)(2,1)S(1)} %bitcast.30, f32[2048,256]{0,1:T(8,128)} %all-reduce.7.cloned.1.call-done), kind=kOutput, calls=%fused_computation.81 | convolution fusion | flops 2418212864 | bytes 13893632 | tf_op jit(solution)/shard_map/dot_general | solution.py:120
  (48 shorter events, 25.6 us)
Async XLA Ops:
  7.2 12.9 %copy-start.4 = (s32[64]{0:T(128)S(1)}, s32[64]{0:T(128)}, u32[]{:S(2)}) copy-start(s32[64]{0:T(128)} %param.12) | copy-start | bytes 772
  7.2 109.8 %collective-permute-start = (bf16[32,6,48,64]{3,2,1,0:T(8,128)(2,1)}, bf16[32,6,48,64]{3,2,1,0:T(8,128)(2,1)}, u32[]{:S(2)}, u32[]{:S(2)}) collective-permute-start(bf16[32,6,48,64]{3,2,1,0:T(8,128)(2,1)} %param.8), channel_id=1, source_target_pairs={{0,1},{1,2},{2,3},{3,4},{4,5},{5,6},{6,7},{7,8},{8,9},{9,10},{10,1... | collective-permute-start | bytes 3538952 | tf_op jit(solution)/shard_map/ppermute | solution.py:31
  8.8 108.2 %collective-permute-start.1 = (bf16[32,6,48,64]{3,2,1,0:T(8,128)(2,1)}, bf16[32,6,48,64]{3,2,1,0:T(8,128)(2,1)}, u32[]{:S(2)}, u32[]{:S(2)}) collective-permute-start(bf16[32,6,48,64]{3,2,1,0:T(8,128)(2,1)} %param.8), channel_id=1, source_target_pairs={{1,0},{2,1},{3,2},{4,3},{5,4},{6,5},{7,6},{8,7},{9,8},{10,9},{11,1... | collective-permute-start | bytes 3538952 | tf_op jit(solution)/shard_map/ppermute | solution.py:32
  15.7 9.1 %copy-start.5 = (s32[64]{0:T(128)S(1)}, s32[64]{0:T(128)}, u32[]{:S(2)}) copy-start(s32[64]{0:T(128)} %param.13) | copy-start | bytes 772
  15.7 11.4 %copy-start.2 = (f32[64,128]{1,0:T(8,128)S(1)}, f32[64,128]{1,0:T(8,128)}, u32[]{:S(2)}) copy-start(f32[64,128]{1,0:T(8,128)} %param.10) | copy-start | bytes 98308
  20.0 13.5 %copy-start = (bf16[32,6,48,64]{3,2,1,0:T(8,128)(2,1)S(1)}, bf16[32,6,48,64]{3,2,1,0:T(8,128)(2,1)}, u32[]{:S(2)}) copy-start(bf16[32,6,48,64]{3,2,1,0:T(8,128)(2,1)} %param.8) | copy-start | bytes 3538948
  27.7 56.8 %collective-permute-start.2 = (f32[32,32]{1,0:T(8,128)S(1)}, f32[32,32]{1,0:T(8,128)S(1)}, u32[]{:S(2)}, u32[]{:S(2)}) collective-permute-start(f32[32,32]{1,0:T(8,128)S(1)} %get-tuple-element.39), channel_id=1, source_target_pairs={{0,1},{1,2},{2,3},{3,4},{4,5},{5,6},{6,7},{7,8},{8,9},{9,10},{10,1... | collective-permute-start | bytes 12296 | tf_op jit(solution)/shard_map/ppermute | solution.py:31
  27.8 56.8 %collective-permute-start.3 = (f32[32,32]{1,0:T(8,128)S(1)}, f32[32,32]{1,0:T(8,128)S(1)}, u32[]{:S(2)}, u32[]{:S(2)}) collective-permute-start(f32[32,32]{1,0:T(8,128)S(1)} %get-tuple-element.40), channel_id=1, source_target_pairs={{1,0},{2,1},{3,2},{4,3},{5,4},{6,5},{7,6},{8,7},{9,8},{10,9},{11,1... | collective-permute-start | bytes 12296 | tf_op jit(solution)/shard_map/ppermute | solution.py:32
  79.9 4.7 copy-start.3
  84.6 12.9 %collective-permute-start.4 = (f32[32,32]{1,0:T(8,128)S(1)}, f32[32,32]{1,0:T(8,128)S(1)}, u32[]{:S(2)}, u32[]{:S(2)}) collective-permute-start(f32[32,32]{1,0:T(8,128)S(1)} %fusion.53), channel_id=1, source_target_pairs={{0,1},{1,2},{2,3},{3,4},{4,5},{5,6},{6,7},{7,8},{8,9},{9,10},{10,1... | collective-permute-start | bytes 12296 | tf_op jit(solution)/shard_map/ppermute | solution.py:31
  84.7 12.9 %collective-permute-start.5 = (f32[32,32]{1,0:T(8,128)S(1)}, f32[32,32]{1,0:T(8,128)S(1)}, u32[]{:S(2)}, u32[]{:S(2)}) collective-permute-start(f32[32,32]{1,0:T(8,128)S(1)} %fusion.53), channel_id=1, source_target_pairs={{1,0},{2,1},{3,2},{4,3},{5,4},{6,5},{7,6},{8,7},{9,8},{10,9},{11,1... | collective-permute-start | bytes 12296 | tf_op jit(solution)/shard_map/ppermute | solution.py:32
  117.0 8.1 %copy-start.1 = (f32[6,48,64]{2,1,0:T(8,128)S(1)}, f32[6,48,64]{2,1,0:T(8,128)}, u32[]{:S(2)}) copy-start(f32[6,48,64]{2,1,0:T(8,128)} %param.9) | copy-start | bytes 221188
  291.6 20.7 %all-to-all-start = ((bf16[8,2,36864]{2,1,0:T(2,128)(2,1)}), bf16[8,2,36864]{2,1,0:T(2,128)(2,1)S(1)}, u32[]{:S(2)}, u32[]{:S(2)}) async-start(bf16[8,2,36864]{2,1,0:T(2,128)(2,1)} %reshape.59), calls=%async_computation | async-start | bytes 2359296 | tf_op jit(solution)/shard_map/all_to_all | solution.py:103
  296.5 188.8 %all-reduce.5.cloned.1.call-start = ((), (), s32[]{:S(2)}) async-start(), calls=%async_computation.1 | async-start | bytes 4194304 | tf_op jit(solution)/shard_map/psum | solution.py:20
  333.0 219.9 %all-reduce.7.cloned.1.call-start = ((), (), s32[]{:S(2)}) async-start(), calls=%async_computation.2 | async-start | bytes 4194304 | tf_op jit(solution)/shard_map/psum | solution.py:21
Sparse Core Ops, SparseCore 0:
  333.1 152.0 all-reduce.4
  487.7 65.1 all-reduce.6
